TPU v7x, 128 devices: a whole 4x4x4 slice. The times are simulated.
128 devices in a mesh: node: 16 (over y, x_hi, core), local: 8 (over z, x_lo).
Axes of the slice: x: 4 (x_hi: 2, x_lo: 2; x = x_hi * 2 + x_lo), y: 4, z: 4, core: 2. Of those that a mesh axis runs over, the one named last changes fastest.
Arguments:
- tokens: bfloat16 [16384, 4096], P(('node', 'local')), may hold values from -8 to 8
- norm_gain: bfloat16 [4096], replicated, may hold values from 0.25 to 1.75
- routes: int32 [16384, 8], P(('node', 'local')), may hold values from 0 to 127, as said below
- route_gates: float32 [16384, 8], P(('node', 'local')), may hold values from 0.35 to 1
- placement: int32 [128], replicated, may hold values from 0 to 127, each once
- gate_weight: bfloat16 [128, 4096, 768], P(('node', 'local')), may hold values from -0.09375 to 0.09375
- up_weight: bfloat16 [128, 4096, 768], P(('node', 'local')), may hold values from -0.09375 to 0.09375
- down_weight: bfloat16 [128, 768, 4096], P(('node', 'local')), may hold values from -0.21875 to 0.21875
Outputs:
- moe_output: bfloat16 [16384, 4096], P(('node', 'local'))
Inputs may be any that keep to these rules, and one draw needn't show every extreme that they name: `routes`: each token names 8 different experts. In every aligned block of 32 tokens of one device, each expert is named at most 3 times; at every block position some expert is named exactly 3 times by that block of every device.
All inputs are finite; a program needn't handle non-finite values.
Results may differ from a plain program's by a relative error of at most 0.0076.
Values may be sent and summed in bfloat16 or wider, within the bound.
A program may use at most 128 MiB of HBM per device.

v0:
```python
import jax
import jax.numpy as jnp
import numpy as np
from jax import lax
from jax.experimental import pallas as pl
from jax.experimental.pallas import tpu as pltpu
from jax.sharding import PartitionSpec as P

MESH = pl.DeviceIdType.MESH
BLOCK_TOK = 32
CAP = 3
EPSILON = 1e-06
SIDE = 4
TOK = 128
TOPK = 8
D = 4096
HID = 768
SLOTS = 12
UNIT = 2 * SLOTS
ROLES = (("x", "y", "z"), ("y", "z", "x"), ("z", "x", "y"))
WIDTH = (1536, 1280, 1280)
START = (0, 1536, 2816)
HALF = tuple(w // 2 for w in WIDTH)
WIDE = max(HALF)
STRIDE = {"x": 16, "y": 4, "z": 1}
STEPS = (0, -1, 1, 2)
RETURNS = {
    (0, 0): (0, 0), (0, 1): (0, 0),
    (1, 0): (2, 0), (1, 1): (1, -1),
    (2, 0): (1, 1), (2, 1): (2, 0),
    (3, 0): (3, -1), (3, 1): (3, 1),
}
VMEM_LIMIT = 62 << 20


def position():
    node, local = lax.axis_index("node"), lax.axis_index("local")
    return {
        "x": (node // 2) % 2 * 2 + local % 2,
        "y": node // 4,
        "z": local // 2,
        "core": node % 2,
    }


def device(at):
    node = (at["y"] * 2 + at["x"] // 2) * 2 + at["core"]
    return node, at["z"] * 2 + at["x"] % 2


def step_on(value, by):
    return (value + by + SIDE) % SIDE


def moved(at, axis, by, core=None, axis2=None, by2=0):
    new = dict(at)
    new[axis] = step_on(at[axis], by)
    if axis2 is not None:
        new[axis2] = step_on(at[axis2], by2)
    if core is not None:
        new["core"] = core
    return device(new)


def greet(at):
    barrier = pltpu.get_barrier_semaphore()
    other = 1 - at["core"]
    partners = [moved(at, "x", 0, other)]
    for _, axis_b, axis_c in ROLES:
        for by in (1, -1, 2):
            for core in (at["core"], other):
                partners.append(moved(at, axis_c, by, core))
                for side in (1, -1):
                    partners.append(moved(at, axis_c, by, core, axis_b, side))
    for partner in partners:
        pl.semaphore_signal(barrier, inc=1, device_id=partner, device_id_type=MESH)
    pl.semaphore_wait(barrier, len(partners))


def remote(src, dst, send, recv, target):
    pltpu.make_async_remote_copy(
        src_ref=src, dst_ref=dst, send_sem=send, recv_sem=recv, device_id=target, device_id_type=MESH
    ).start()


def local_copy(src, dst, sem):
    pltpu.make_async_copy(src, dst, sem).start()


def await_bytes(ref, sem):
    pltpu.make_async_copy(ref, ref, sem).wait()


def tiles(width):
    return [(at, min(256, width - at)) for at in range(0, width, 256)]


def kernel(
    tokens, gain, own_meta, pattern, gate_w, up_w, down_w,
    result, in0, in1, in2, back0, back1, back2, land0, land1, land2,
    g0, g1, g2, n0, n1, n2, out0, out1, out2, st0, st1, st2, m0, m1, m2, k0, k1, k2,
    stage, share, rows_bf, weights, acc, own2, low, r0, r1, r2, last, end0, end1, end2,
    w_sem, own_sem, core_send, core_recv, meta_send, meta_recv, a_send, a_recv, ah_send, ah_recv, b_send, b_recv,
    row_send, row_recv, stage_sem, back_send, back_recv, sum_send, sum_recv, c_send, c_recv, end_send, end_recv,
):
    at = position()
    core = at["core"]
    other = 1 - core
    groups = range(3)
    gathered, near, outbox, inbox = (g0, g1, g2), (n0, n1, n2), (out0, out1, out2), (in0, in1, in2)
    staged, metas, near_metas = (st0, st1, st2), (m0, m1, m2), (k0, k1, k2)
    backbox, landed, arrived, ends = (back0, back1, back2), (land0, land1, land2), (r0, r1, r2), (end0, end1, end2)
    local_copy(gate_w.at[0], weights.at[:, pl.ds(0, HID)], w_sem.at[0])
    local_copy(up_w.at[0], weights.at[:, pl.ds(HID, HID)], w_sem.at[1])

    @pl.loop(0, TOK // 16)
    def _(step):
        rows = pl.ds(pl.multiple_of(step * 16, 16), 16)
        values = tokens[rows, :].astype(jnp.float32)
        rescale = lax.rsqrt(jnp.sum(values * values, axis=-1, keepdims=True) * (1.0 / D) + EPSILON)
        normed = (values * rescale * gain[...].astype(jnp.float32)).astype(jnp.bfloat16)
        for g in groups:
            for h in range(2):
                low_at = START[g] + h * HALF[g]
                staged[g][h, rows, :] = normed[:, low_at : low_at + HALF[g]]

    greet(at)
    for g in groups:
        a = at[ROLES[g][0]]
        metas[g][a, core] = own_meta[...]
        remote(metas[g].at[a, core], metas[g].at[a, core], meta_send.at[g, 0], meta_recv.at[g, 0], moved(at, "x", 0, other))
        remote(staged[g].at[other], gathered[g].at[a, core], core_send.at[g], core_recv.at[g], moved(at, "x", 0, other))
        local_copy(staged[g].at[core], gathered[g].at[a, core], own_sem.at[g])

    def spread(g, order, a_from):
        pair = a_from // 2
        remote(gathered[g].at[a_from], near[g].at[pair, a_from % 2], b_send.at[g, order], b_recv.at[g, pair],
               moved(at, ROLES[g][1], 1 - 2 * pair))

    for g in groups:
        axis_a = ROLES[g][0]
        a = at[axis_a]
        await_bytes(gathered[g].at[a, core], own_sem.at[g])
        await_bytes(gathered[g].at[a, core], core_recv.at[g])
        for way, by in enumerate((1, -1)):
            remote(gathered[g].at[a], gathered[g].at[a], a_send.at[g, way], a_recv.at[g, way], moved(at, axis_a, by))
        await_bytes(metas[g].at[a, core], meta_recv.at[g, 0])
        for by in (1, -1, 2):
            remote(metas[g].at[a], metas[g].at[a], meta_send.at[g, 1], meta_recv.at[g, 1], moved(at, axis_a, by))
    for g in groups:
        spread(g, 0, at[ROLES[g][0]])
    for g in groups:
        await_bytes(metas[g].at[pl.ds(0, 3)], meta_recv.at[g, 1])
        for pair in range(2):
            remote(metas[g].at[pl.ds(2 * pair, 2)], near_metas[g].at[pair], meta_send.at[g, 2], meta_recv.at[g, 2],
                   moved(at, ROLES[g][1], 1 - 2 * pair))

    @pl.loop(0, 64)
    def _(unit):
        acc[pl.ds(pl.multiple_of(unit * UNIT, 8), UNIT), :] = jnp.zeros((UNIT, 2 * HID), jnp.float32)

    for way, by in enumerate((1, -1)):
        for g in groups:
            axis_a = ROLES[g][0]
            a_from = step_on(at[axis_a], -by)
            await_bytes(gathered[g].at[a_from], a_recv.at[g, way])
            remote(gathered[g].at[a_from, way], gathered[g].at[a_from, way], ah_send.at[g, way], ah_recv.at[g, way],
                   moved(at, axis_a, by))
            spread(g, 1 + way, a_from)
    for g in groups:
        a_from = step_on(at[ROLES[g][0]], 2)
        for way in range(2):
            await_bytes(gathered[g].at[a_from, way], ah_recv.at[g, way])
        spread(g, 3, a_from)

    def line_base(g, by):
        _, axis_b, axis_c = ROLES[g]
        spot = dict(at)
        spot[axis_b] = step_on(at[axis_b], by)
        spot[axis_c] = 0
        spot["core"] = 0
        node, local = device(spot)
        return ((node * 8 + local) * (4 * SLOTS)).astype(jnp.float32)

    def meta_of(g, is_near, pair, index, k):
        return near_metas[g][pair, index, k] if is_near else metas[g][pair * 2 + index, k]

    def column_codes(g, is_near, pair):
        return jnp.concatenate(
            [meta_of(g, is_near, pair, i, k)[:TOPK] * 4.0 + float(i * 2 + k) for i in range(2) for k in range(2)], axis=1
        )

    def pick_and_send(g, kind):
        _, axis_b, axis_c = ROLES[g]
        is_near = kind >= 2

        @pl.loop(0, 2)
        def _(pair):
            if kind == 3:
                await_bytes(near[g].at[pair], b_recv.at[g, pair])
            ahead = 1 - 2 * pair
            by_b = (0, -ahead, 0, ahead)[kind]
            order = (0, 2 - pair, 1 + pair, 3)[kind]
            codes = column_codes(g, is_near, pair)
            rows = pattern[g] + line_base(g, by_b)
            found = rows == codes[0:1]
            for k in range(1, TOPK):
                found = jnp.logical_or(found, rows == codes[k : k + 1])
            share[0:384, 0:512] = jnp.where(found, 1.0, 0.0).astype(jnp.bfloat16)
            for low_at, size in tiles(HALF[g]):
                span = slice(low_at, low_at + size)
                if is_near:
                    block = near[g][pair, :, :, :, span]
                else:
                    block = gathered[g][pl.ds(pair * 2, 2), :, :, span]
                picked = jnp.dot(share[0:384, 0:512], block.reshape(512, size), preferred_element_type=jnp.float32)
                outbox[g][kind * 2 + pair, :, :, span] = picked.astype(jnp.bfloat16).reshape(8, 48, size)
            c = at[axis_c]
            for by in (1, -1, 2, 0):
                c_to = step_on(c, by)
                for k in range(2):
                    core_to = (core + k) % 2
                    box = outbox[g].at[kind * 2 + pair, c_to * 2 + core_to]
                    slot = inbox[g].at[order, core, c, pair]
                    if by == 0 and k == 0 and kind in (0, 2):
                        local_copy(box, slot, row_recv.at[g, order])
                    else:
                        remote(box, slot, row_send.at[g, kind], row_recv.at[g, order],
                               moved(at, axis_c, by, core_to, axis_b, by_b))

    def multiply(g, order):
        axis_a, axis_b, axis_c = ROLES[g]
        b_from = step_on(at[axis_b], STEPS[order])
        await_bytes(inbox[g].at[order], row_recv.at[g, order])
        copy = pltpu.make_async_copy(inbox[g].at[order], stage.at[:, :, :, :, pl.ds(0, HALF[g])], stage_sem.at[0])
        copy.start()
        copy.wait()

        @pl.loop(0, 2 * HID // 256)
        def _(tile):
            columns = pl.ds(pl.multiple_of(tile * 256, 256), 256)
            total = None
            for h in range(2):
                rows = stage[h, :, :, :, 0 : HALF[g]].reshape(384, HALF[g])
                part = jnp.dot(rows, weights[START[g] + h * HALF[g] : START[g] + (h + 1) * HALF[g], columns],
                               preferred_element_type=jnp.float32)
                total = part if total is None else total + part
            for c in range(SIDE):
                for a in range(SIDE):
                    unit = a * STRIDE[axis_a] + b_from * STRIDE[axis_b] + c * STRIDE[axis_c]
                    low_at = (c * SIDE + a) * UNIT
                    acc[pl.ds(pl.multiple_of(unit * UNIT, 8), UNIT), columns] += total[low_at : low_at + UNIT]

    for kind in (0, 1):
        for g in groups:
            pick_and_send(g, kind)
    for g in groups:
        await_bytes(near_metas[g], meta_recv.at[g, 2])
    for kind in (3, 2):
        for g in groups:
            pick_and_send(g, kind)
    await_bytes(weights.at[:, pl.ds(0, HID)], w_sem.at[0])
    await_bytes(weights.at[:, pl.ds(HID, HID)], w_sem.at[1])

    def down_of(g):
        return weights.at[pl.ds(g * HID, HID), pl.ds(0, WIDTH[g])]

    def fetch_down(g):
        local_copy(down_w.at[0, :, pl.ds(START[g], WIDTH[g])], down_of(g), w_sem.at[2 + g])

    for order in (0, 3, 1, 2):
        for g in groups:
            multiply(g, order)
            if order == 2 and g == 0:
                fetch_down(0)
                fetch_down(1)
            if order == 2 and g == 1:
                fetch_down(2)

    @pl.loop(0, 64)
    def _(unit):
        rows = pl.ds(pl.multiple_of(unit * UNIT, 8), UNIT)
        gate, up = acc[rows, 0:HID], acc[rows, HID : 2 * HID]
        hidden = gate / (1.0 + jnp.exp(-gate)) * up
        acc[rows, 0:HID] = hidden.astype(jnp.bfloat16).astype(jnp.float32)

    for g in groups:
        for kind in range(4):
            count = 7 if kind in (0, 2) else 8
            await_bytes(outbox[g].at[pl.ds(0, 2), pl.ds(0, count)], row_send.at[g, kind])
    for g in groups:
        await_bytes(down_of(g), w_sem.at[2 + g])

    def expand_and_send(g, order):
        axis_a, axis_b, axis_c = ROLES[g]
        b_to = step_on(at[axis_b], STEPS[order])
        for c in range(SIDE):
            units = [
                acc[pl.ds(pl.multiple_of(
                    (a * STRIDE[axis_a] + b_to * STRIDE[axis_b] + c * STRIDE[axis_c]) * UNIT, 8), UNIT), 0:HID]
                for a in range(SIDE)
            ]
            rows_bf[c * 96 : (c + 1) * 96, :] = jnp.concatenate(units, axis=0).astype(jnp.bfloat16)

        @pl.loop(0, 2)
        def _(h):
            for low_at, size in tiles(HALF[g]):
                columns = pl.ds(pl.multiple_of(h * HALF[g] + low_at, 128), size)
                made = jnp.dot(rows_bf[...], weights[g * HID : (g + 1) * HID, columns], preferred_element_type=jnp.float32)
                made = made.astype(jnp.bfloat16).reshape(SIDE, 2, 48, size)
                for pair in range(2):
                    outbox[g][order * 2 + pair, pl.ds(h * SIDE, SIDE), :, low_at : low_at + size] = made[:, pair]

        c = at[axis_c]
        for pair in range(2):
            kind, by_b = RETURNS[order, pair]
            for by in (1, -1, 2, 0):
                c_to = step_on(c, by)
                for k in range(2):
                    core_to = (core + k) % 2
                    box = outbox[g].at[order * 2 + pair, core_to * SIDE + c_to]
                    slot = backbox[g].at[kind // 2, pair, kind % 2, c * 2 + core]
                    sem = back_recv.at[g, kind // 2, pair]
                    if by == 0 and k == 0 and by_b == 0:
                        local_copy(box, slot, sem)
                    else:
                        remote(box, slot, back_send.at[g, order, pair], sem, moved(at, axis_c, by, core_to, axis_b, by_b))

    def load(source, target, sem):
        copy = pltpu.make_async_copy(source, target, sem)
        copy.start()
        copy.wait()

    def combine(g, is_near, place):
        view = stage.reshape(2, 8, 48, WIDE).at[:, :, :, pl.ds(0, HALF[g])]

        @pl.loop(0, 2)
        def _(pair):
            ahead = 1 - 2 * pair
            codes = column_codes(g, is_near, pair)
            scale = jnp.concatenate(
                [meta_of(g, is_near, pair, i, k)[TOPK:] for i in range(2) for k in range(2)], axis=1
            )
            for side, by in enumerate((0, ahead if is_near else -ahead)):
                rows = pattern[g] + line_base(g, by)
                total = jnp.where(rows == codes[0:1], scale[0:1], 0.0)
                for k in range(1, TOPK):
                    total = jnp.where(rows == codes[k : k + 1], scale[k : k + 1], total)
                share[:, side * 384 : (side + 1) * 384] = total.T.astype(jnp.bfloat16)
            await_bytes(backbox[g].at[int(is_near), pair], back_recv.at[g, int(is_near), pair])
            load(backbox[g].at[int(is_near), pair], view, stage_sem.at[0])
            if not is_near:
                await_bytes(landed[g].at[pair], sum_recv.at[g, pair])
                load(landed[g].at[pair], low.at[:, :, :, pl.ds(0, HALF[g])], stage_sem.at[1])
            for low_at, size in tiles(HALF[g]):
                block = stage[:, :, :, :, low_at : low_at + size].reshape(768, size)
                mixed = jnp.dot(share[...], block, preferred_element_type=jnp.float32)
                place(pair, low_at, size, mixed.reshape(2, 2, TOK, size))

    def pass_on(g):
        def place(pair, low_at, size, block):
            near[g][pair, :, :, :, low_at : low_at + size] = block.astype(jnp.bfloat16)

        combine(g, True, place)
        for pair in range(2):
            remote(near[g].at[pair], landed[g].at[pair], sum_send.at[g, pair], sum_recv.at[g, pair],
                   moved(at, ROLES[g][1], 2 * pair - 1))

    def own_at(g, chip, half):
        rows = pl.ds(pl.multiple_of((chip * 2 + half) * TOK, TOK), TOK)
        if g == 2:
            return own2, rows, 0
        return acc, rows, g * WIDE

    def settled(g, chip, half):
        ref, rows, column = own_at(g, chip, half)
        return ref[rows, column : column + HALF[g]]

    def home(g):
        axis_a = ROLES[g][0]

        def place(pair, low_at, size, block):
            for i in range(2):
                for half in range(2):
                    ref, rows, column = own_at(g, pair * 2 + i, half)
                    value = block[i, half] + low[i, half, :, low_at : low_at + size].astype(jnp.float32)
                    ref[rows, column + low_at : column + low_at + size] = value

        combine(g, False, place)
        opposite = step_on(at[axis_a], 2)
        for half, by in enumerate((1, -1)):
            gathered[g][0, half] = settled(g, opposite, half).astype(jnp.bfloat16)
            remote(gathered[g].at[0, half], arrived[g].at[half], c_send.at[g, half], c_recv.at[g, half],
                   moved(at, axis_a, by))

    def relay(g):
        axis_a = ROLES[g][0]
        for half_in, by in enumerate((1, -1)):
            a_to = step_on(at[axis_a], by)
            await_bytes(arrived[g].at[half_in], c_recv.at[g, half_in])
            for half in range(2):
                value = settled(g, a_to, half)
                if half == half_in:
                    value = value + arrived[g][half_in].astype(jnp.float32)
                gathered[g][1 + half_in, half] = value.astype(jnp.bfloat16)
            remote(gathered[g].at[1 + half_in], arrived[g].at[pl.ds(2 + 2 * half_in, 2)], c_send.at[g, 2 + half_in],
                   c_recv.at[g, 2 + half_in], moved(at, axis_a, by))

    def finish(g):
        for index in range(2):
            await_bytes(arrived[g].at[pl.ds(2 + 2 * index, 2)], c_recv.at[g, 2 + index])
        for half in range(2):
            value = settled(g, at[ROLES[g][0]], half) + arrived[g][2 + half].astype(jnp.float32)
            value = value + arrived[g][4 + half].astype(jnp.float32)
            last[half, :, START[g] // 2 : START[g] // 2 + HALF[g]] = value.astype(jnp.bfloat16)
        span = pl.ds(START[g] // 2, HALF[g])
        remote(last.at[other, :, span], ends[g], end_send.at[g], end_recv.at[g], moved(at, "x", 0, other))

    for order in (3, 1, 2, 0):
        for g in groups:
            expand_and_send(g, order)
    for g in groups:
        pass_on(g)
    for g in groups:
        for way in range(2):
            await_bytes(gathered[g].at[0], a_send.at[g, way])
            await_bytes(gathered[g].at[0, 0], ah_send.at[g, way])
        for order in range(4):
            await_bytes(gathered[g].at[0], b_send.at[g, order])
    home(0)
    home(1)
    relay(0)
    home(2)
    relay(1)
    relay(2)
    for g in groups:
        finish(g)
    for g in groups:
        mine = last[core, :, START[g] // 2 : START[g] // 2 + HALF[g]]
        await_bytes(ends[g], end_recv.at[g])
        theirs = ends[g][...]
        result[:, START[g] : START[g] + HALF[g]] = jnp.where(core == 0, mine, theirs)
        result[:, START[g] + HALF[g] : START[g] + WIDTH[g]] = jnp.where(core == 0, theirs, mine)
    for g in groups:
        await_bytes(metas[g].at[0, 0], meta_send.at[g, 0])
        await_bytes(metas[g].at[pl.ds(0, 3)], meta_send.at[g, 1])
        await_bytes(near_metas[g], meta_send.at[g, 2])
        await_bytes(staged[g].at[0], core_send.at[g])
        for order in range(4):
            for pair in range(2):
                count = 7 if RETURNS[order, pair][1] == 0 else 8
                await_bytes(outbox[g].at[0, pl.ds(0, count)], back_send.at[g, order, pair])
        for index in range(2):
            await_bytes(near[g].at[index], sum_send.at[g, index])
            await_bytes(arrived[g].at[index], c_send.at[g, index])
            await_bytes(arrived[g].at[pl.ds(0, 2)], c_send.at[g, 2 + index])
        await_bytes(ends[g], end_send.at[g])


def row_pattern():
    row = np.arange(384)
    line, core, inner = row // 96, row // 48 % 2, row % 48
    tables = []
    for roles in ROLES:
        spot = {"x": 0 * line, "y": 0 * line, "z": 0 * line, "core": core}
        spot[roles[2]] = line
        node, local = device(spot)
        tables.append(((node * 8 + local) * SLOTS + inner % SLOTS) * 4 + inner // SLOTS)
    return jnp.asarray(np.stack(tables)[:, :, None].astype(np.float32))


def body(tokens, norm_gain, routes, route_gates, placement, gate_weight, up_weight, down_weight):
    experts = placement.shape[0]
    blocks = TOK // BLOCK_TOK
    bf16, f32 = jnp.bfloat16, jnp.float32
    combine_weight = (route_gates / jnp.sum(route_gates, axis=-1, keepdims=True)).astype(bf16)
    expert_ids = jnp.arange(experts, dtype=jnp.int32)
    holder = jnp.sum(jnp.where(placement[None, :] == expert_ids[:, None], expert_ids[None, :], 0), axis=1)
    one_hot = routes[:, :, None] == expert_ids
    target = jnp.sum(jnp.where(one_hot, holder, 0), axis=-1)
    named = jnp.any(one_hot, axis=1).astype(f32).reshape(blocks, BLOCK_TOK, experts)
    before = jnp.einsum("ts,bse->bte", jnp.tril(jnp.ones((BLOCK_TOK, BLOCK_TOK), f32), -1), named)
    position_in = jnp.sum(jnp.where(one_hot, before.reshape(TOK, 1, experts), 0.0), axis=-1)
    block = (jnp.arange(TOK) // BLOCK_TOK).astype(f32)[:, None]
    code = target.astype(f32) * SLOTS + block * CAP + position_in
    own_meta = jnp.concatenate([code.T, combine_weight.astype(f32).T], axis=0)

    vmem, hbm = pl.BlockSpec(memory_space=pltpu.VMEM), pl.BlockSpec(memory_space=pltpu.HBM)
    dma = pltpu.SemaphoreType.DMA
    shape = jax.ShapeDtypeStruct
    meta = (2, 2 * TOPK, TOK)

    def each(*dims):
        return [pltpu.VMEM((*dims, h), bf16) for h in HALF]

    result, *_ = pl.pallas_call(
        kernel,
        out_shape=[shape((TOK, D), bf16)]
        + [shape((4, 2, SIDE, 2, 48, h), bf16) for h in HALF]
        + [shape((2, 2, 2, 8, 48, h), bf16) for h in HALF]
        + [shape((2, 2, 2, TOK, h), bf16) for h in HALF],
        in_specs=[vmem] * 4 + [hbm] * 3,
        out_specs=[vmem] + [hbm] * 9,
        scratch_shapes=each(SIDE, 2, TOK)
        + each(2, 2, 2, TOK)
        + each(8, 8, 48)
        + each(2, TOK)
        + [pltpu.VMEM((SIDE, *meta), f32)] * 3
        + [pltpu.VMEM((2, 2, *meta), f32)] * 3
        + [
            pltpu.VMEM((2, SIDE, 2, 48, WIDE), bf16),
            pltpu.VMEM((512, 768), bf16),
            pltpu.VMEM((384, HID), bf16),
            pltpu.VMEM((D, 2 * HID), bf16),
            pltpu.VMEM((64 * UNIT, 2 * HID), f32),
            pltpu.VMEM((SIDE * 2 * TOK, HALF[2]), f32),
            pltpu.VMEM((2, 2, TOK, WIDE), bf16),
        ]
        + each(6, TOK)
        + [pltpu.VMEM((2, TOK, D // 2), bf16)]
        + each(TOK)
        + [
            dma((5,)), dma((3,)), dma((3,)), dma((3,)), dma((3, 3)), dma((3, 3)),
            dma((3, 2)), dma((3, 2)), dma((3, 2)), dma((3, 2)), dma((3, 4)), dma((3, 2)),
            dma((3, 4)), dma((3, 4)), dma((2,)), dma((3, 4, 2)), dma((3, 2, 2)), dma((3, 2)), dma((3, 2)),
            dma((3, 4)), dma((3, 4)), dma((3,)), dma((3,)),
        ],
        compiler_params=pltpu.CompilerParams(collective_id=0, has_side_effects=True, vmem_limit_bytes=VMEM_LIMIT),
        name="experts",
    )(tokens, norm_gain[None, :], own_meta, row_pattern(), gate_weight, up_weight, down_weight)
    return result


def solution(mesh):
    rows = P(("node", "local"), None)
    whole = P(("node", "local"), None, None)
    in_specs = (rows, P(), rows, rows, P(), whole, whole, whole)
    return jax.shard_map(body, mesh=mesh, in_specs=in_specs, out_specs=rows, check_vma=False)
```

profile of v0, /device:TPU:35, one launch (start us, length us, event | category | flops | bytes accessed | tf_op | source)
XLA Modules:
  0.0 317.8 jit_solution(17534868242493657480)
XLA Ops:
  0.0 0.8 select_reduce_fusion.2
  0.8 0.7 reduce_sum.39
  1.5 1.3 broadcast_in_dim.51.gain
  2.8 0.8 copy.11
  3.6 0.3 fusion
  3.8 0.2 fusion.1
  4.0 0.4 select_reduce_fusion
  4.5 2.4 select_reduce_fusion.1
  6.9 0.7 convert_bitcast_fusion
  7.6 0.6 pad_maximum_fusion.own_meta
  8.2 307.1 %experts.1 = (bf16[128,4096]{1,0:T(8,128)(2,1)}, bf16[4,2,4,2,48,768]{5,4,3,2,1,0:T(8,128)(2,1)}, bf16[4,2,4,2,48,640]{5,4,3,2,1,0:T(8,128)(2,1)}, bf16[4,2,4,2,...) custom-call(bf16[128,4096]{1,0:T(8,128)(2,1)} %tokens.1, ...), custom_call_target="tpu_custom_call" | custom-call | tf_op jit(solution)/shard_map/experts/pallas_call | solution.py:496
  315.3 2.3 copy.15
  (4 shorter events, 0.1 us)
where the time goes:
time: 322 us; the launch traced here: 318 us
  Pallas kernels  307 us (95%)
  other arithmetic  5.82 us (2%)
  local copies, waits for them, and re-layouts  4.48 us (1%)
    pallas_call x1, Pallas kernels, body(): pl.pallas_call(kernel, out_shape=[shape((TOK, D), bf16)] + [shape((4, 2,...  307 us

commit v1 on v0

--- a/solution.py
+++ b/solution.py
@@ -62,8 +62,7 @@
     return device(new)
 
 
-def greet(at):
-    barrier = pltpu.get_barrier_semaphore()
+def greet(at, barrier):
     other = 1 - at["core"]
     partners = [moved(at, "x", 0, other)]
     for _, axis_b, axis_c in ROLES:
@@ -74,7 +73,7 @@
                     partners.append(moved(at, axis_c, by, core, axis_b, side))
     for partner in partners:
         pl.semaphore_signal(barrier, inc=1, device_id=partner, device_id_type=MESH)
-    pl.semaphore_wait(barrier, len(partners))
+    return len(partners)
 
 
 def remote(src, dst, send, recv, target):
@@ -95,11 +94,34 @@
     return [(at, min(256, width - at)) for at in range(0, width, 256)]
 
 
+def slot_codes(routes, packed, placement):
+    side = (TOK, TOK)
+    down = lax.broadcasted_iota(jnp.int32, side, 0)
+    across = lax.broadcasted_iota(jnp.int32, side, 1)
+    earlier = jnp.logical_and(down < across, down // BLOCK_TOK == across // BLOCK_TOK)
+    place = jnp.broadcast_to(placement[...].astype(jnp.float32), side).T
+    index = down.astype(jnp.float32)
+    columns = [jnp.broadcast_to(routes[:, k : k + 1].astype(jnp.float32), side) for k in range(TOPK)]
+    block = (across[0:1] // BLOCK_TOK * CAP).astype(jnp.float32)
+    codes = []
+    for k in range(TOPK):
+        wanted = packed[k : k + 1]
+        holder = jnp.sum(jnp.where(place == wanted, index, 0.0), axis=0, keepdims=True)
+        same = columns[0] == wanted
+        for column in columns[1:]:
+            same = jnp.logical_or(same, column == wanted)
+        count = jnp.sum(jnp.where(jnp.logical_and(same, earlier), 1.0, 0.0), axis=0, keepdims=True)
+        codes.append(holder * float(SLOTS) + block + count)
+    gates = packed[TOPK:]
+    weight = gates / jnp.sum(gates, axis=0, keepdims=True)
+    return jnp.concatenate(codes + [weight.astype(jnp.bfloat16).astype(jnp.float32)], axis=0)
+
+
 def kernel(
-    tokens, gain, own_meta, pattern, gate_w, up_w, down_w,
+    tokens, gain, routes, packed, placement, lines, gate_w, up_w, down_w,
     result, in0, in1, in2, back0, back1, back2, land0, land1, land2,
     g0, g1, g2, n0, n1, n2, out0, out1, out2, st0, st1, st2, m0, m1, m2, k0, k1, k2,
-    stage, share, rows_bf, weights, acc, own2, low, r0, r1, r2, last, end0, end1, end2,
+    code_box, stage, share, rows_bf, weights, acc, own2, low, r0, r1, r2, last, end0, end1, end2,
     w_sem, own_sem, core_send, core_recv, meta_send, meta_recv, a_send, a_recv, ah_send, ah_recv, b_send, b_recv,
     row_send, row_recv, stage_sem, back_send, back_recv, sum_send, sum_recv, c_send, c_recv, end_send, end_recv,
 ):
@@ -110,6 +132,8 @@
     gathered, near, outbox, inbox = (g0, g1, g2), (n0, n1, n2), (out0, out1, out2), (in0, in1, in2)
     staged, metas, near_metas = (st0, st1, st2), (m0, m1, m2), (k0, k1, k2)
     backbox, landed, arrived, ends = (back0, back1, back2), (land0, land1, land2), (r0, r1, r2), (end0, end1, end2)
+    barrier = pltpu.get_barrier_semaphore()
+    greeted = greet(at, barrier)
     local_copy(gate_w.at[0], weights.at[:, pl.ds(0, HID)], w_sem.at[0])
     local_copy(up_w.at[0], weights.at[:, pl.ds(HID, HID)], w_sem.at[1])
 
@@ -124,13 +148,25 @@
                 low_at = START[g] + h * HALF[g]
                 staged[g][h, rows, :] = normed[:, low_at : low_at + HALF[g]]
 
-    greet(at)
+    pl.semaphore_wait(barrier, greeted)
     for g in groups:
         a = at[ROLES[g][0]]
-        metas[g][a, core] = own_meta[...]
-        remote(metas[g].at[a, core], metas[g].at[a, core], meta_send.at[g, 0], meta_recv.at[g, 0], moved(at, "x", 0, other))
         remote(staged[g].at[other], gathered[g].at[a, core], core_send.at[g], core_recv.at[g], moved(at, "x", 0, other))
         local_copy(staged[g].at[core], gathered[g].at[a, core], own_sem.at[g])
+
+    def ring(g, half, first):
+        axis_a = ROLES[g][0]
+        a = at[axis_a]
+        source = staged[g].at[half] if first else gathered[g].at[a, half]
+        for way, by in enumerate((1, -1)):
+            remote(source, gathered[g].at[a, half], a_send.at[g, way, half], a_recv.at[g, way, half], moved(at, axis_a, by))
+
+    def spread_own(g, half, first):
+        a = at[ROLES[g][0]]
+        pair = a // 2
+        source = staged[g].at[half] if first else gathered[g].at[a, half]
+        remote(source, near[g].at[pair, a % 2, half], b_send.at[g, 0 if first else 4], b_recv.at[g, pair],
+               moved(at, ROLES[g][1], 1 - 2 * pair))
 
     def spread(g, order, a_from):
         pair = a_from // 2
@@ -138,36 +174,49 @@
                moved(at, ROLES[g][1], 1 - 2 * pair))
 
     for g in groups:
+        ring(g, core, True)
+    for g in groups:
+        spread_own(g, core, True)
+    code_box[...] = slot_codes(routes, packed, placement)
+    for g in groups:
+        a = at[ROLES[g][0]]
+        metas[g][a, core] = code_box[...]
+        remote(code_box, metas[g].at[a, core], meta_send.at[g, 0], meta_recv.at[g, 0], moved(at, "x", 0, other))
+    for g in groups:
+        await_bytes(staged[g].at[0], core_recv.at[g])
+        ring(g, other, False)
+    for g in groups:
+        spread_own(g, other, False)
+    for g in groups:
         axis_a = ROLES[g][0]
         a = at[axis_a]
-        await_bytes(gathered[g].at[a, core], own_sem.at[g])
-        await_bytes(gathered[g].at[a, core], core_recv.at[g])
-        for way, by in enumerate((1, -1)):
-            remote(gathered[g].at[a], gathered[g].at[a], a_send.at[g, way], a_recv.at[g, way], moved(at, axis_a, by))
-        await_bytes(metas[g].at[a, core], meta_recv.at[g, 0])
+        await_bytes(code_box, meta_recv.at[g, 0])
         for by in (1, -1, 2):
             remote(metas[g].at[a], metas[g].at[a], meta_send.at[g, 1], meta_recv.at[g, 1], moved(at, axis_a, by))
-    for g in groups:
-        spread(g, 0, at[ROLES[g][0]])
+
+    @pl.loop(0, 64)
+    def _(unit):
+        acc[pl.ds(pl.multiple_of(unit * UNIT, 8), UNIT), :] = jnp.zeros((UNIT, 2 * HID), jnp.float32)
+
+    for way, by in enumerate((1, -1)):
+        for g in groups:
+            axis_a = ROLES[g][0]
+            a_from = step_on(at[axis_a], -by)
+            await_bytes(gathered[g].at[a_from, way], a_recv.at[g, way, way])
+            remote(gathered[g].at[a_from, way], gathered[g].at[a_from, way], ah_send.at[g, way], ah_recv.at[g, way],
+                   moved(at, axis_a, by))
+    for way, by in enumerate((1, -1)):
+        for g in groups:
+            a_from = step_on(at[ROLES[g][0]], -by)
+            await_bytes(gathered[g].at[a_from, 1 - way], a_recv.at[g, way, 1 - way])
+            spread(g, 1 + way, a_from)
     for g in groups:
         await_bytes(metas[g].at[pl.ds(0, 3)], meta_recv.at[g, 1])
         for pair in range(2):
             remote(metas[g].at[pl.ds(2 * pair, 2)], near_metas[g].at[pair], meta_send.at[g, 2], meta_recv.at[g, 2],
                    moved(at, ROLES[g][1], 1 - 2 * pair))
-
-    @pl.loop(0, 64)
-    def _(unit):
-        acc[pl.ds(pl.multiple_of(unit * UNIT, 8), UNIT), :] = jnp.zeros((UNIT, 2 * HID), jnp.float32)
-
-    for way, by in enumerate((1, -1)):
-        for g in groups:
-            axis_a = ROLES[g][0]
-            a_from = step_on(at[axis_a], -by)
-            await_bytes(gathered[g].at[a_from], a_recv.at[g, way])
-            remote(gathered[g].at[a_from, way], gathered[g].at[a_from, way], ah_send.at[g, way], ah_recv.at[g, way],
-                   moved(at, axis_a, by))
-            spread(g, 1 + way, a_from)
-    for g in groups:
+    for g in groups:
+        await_bytes(gathered[g].at[0, 0], own_sem.at[g])
         a_from = step_on(at[ROLES[g][0]], 2)
         for way in range(2):
             await_bytes(gathered[g].at[a_from, way], ah_recv.at[g, way])
@@ -180,15 +229,24 @@
         spot[axis_c] = 0
         spot["core"] = 0
         node, local = device(spot)
-        return ((node * 8 + local) * (4 * SLOTS)).astype(jnp.float32)
+        return ((node * 8 + local) * SLOTS).astype(jnp.float32)
 
     def meta_of(g, is_near, pair, index, k):
         return near_metas[g][pair, index, k] if is_near else metas[g][pair * 2 + index, k]
 
-    def column_codes(g, is_near, pair):
-        return jnp.concatenate(
-            [meta_of(g, is_near, pair, i, k)[:TOPK] * 4.0 + float(i * 2 + k) for i in range(2) for k in range(2)], axis=1
-        )
+    def slot_rows(g, is_near, pair, index, by):
+        both = [meta_of(g, is_near, pair, index, k) for k in range(2)]
+        table = jnp.concatenate(both, axis=1)
+        first = lines[g] + line_base(g, by)
+        slot = jnp.full((8, 2 * TOK), -100.0, jnp.float32)
+        weight = jnp.zeros((8, 2 * TOK), jnp.float32)
+        for k in range(TOPK):
+            offset = table[k : k + 1] - first
+            hit = jnp.logical_and(offset >= 0.0, offset < float(SLOTS))
+            slot = jnp.where(hit, offset, slot)
+            weight = jnp.where(hit, table[TOPK + k : TOPK + k + 1], weight)
+        lane = lax.broadcasted_iota(jnp.int32, (8, 2 * TOK), 1)
+        return slot + jnp.where(lane >= TOK, float(SLOTS), 0.0), weight
 
     def pick_and_send(g, kind):
         _, axis_b, axis_c = ROLES[g]
@@ -201,20 +259,20 @@
             ahead = 1 - 2 * pair
             by_b = (0, -ahead, 0, ahead)[kind]
             order = (0, 2 - pair, 1 + pair, 3)[kind]
-            codes = column_codes(g, is_near, pair)
-            rows = pattern[g] + line_base(g, by_b)
-            found = rows == codes[0:1]
-            for k in range(1, TOPK):
-                found = jnp.logical_or(found, rows == codes[k : k + 1])
-            share[0:384, 0:512] = jnp.where(found, 1.0, 0.0).astype(jnp.bfloat16)
+            number = lax.broadcasted_iota(jnp.int32, (UNIT, 2 * TOK), 0).astype(jnp.float32)
+            for i in range(2):
+                slot, _ = slot_rows(g, is_near, pair, i, by_b)
+                found = [jnp.where(number == slot[d : d + 1], 1.0, 0.0) for d in range(8)]
+                share[0 : 8 * UNIT, i * 256 : (i + 1) * 256] = jnp.concatenate(found, axis=0).astype(jnp.bfloat16)
             for low_at, size in tiles(HALF[g]):
                 span = slice(low_at, low_at + size)
-                if is_near:
-                    block = near[g][pair, :, :, :, span]
-                else:
-                    block = gathered[g][pl.ds(pair * 2, 2), :, :, span]
-                picked = jnp.dot(share[0:384, 0:512], block.reshape(512, size), preferred_element_type=jnp.float32)
-                outbox[g][kind * 2 + pair, :, :, span] = picked.astype(jnp.bfloat16).reshape(8, 48, size)
+                parts = []
+                for i in range(2):
+                    block = near[g][pair, i, :, :, span] if is_near else gathered[g][pair * 2 + i, :, :, span]
+                    picked = jnp.dot(share[0 : 8 * UNIT, i * 256 : (i + 1) * 256], block.reshape(2 * TOK, size),
+                                     preferred_element_type=jnp.float32)
+                    parts.append(picked.reshape(8, UNIT, size))
+                outbox[g][kind * 2 + pair, :, :, span] = jnp.concatenate(parts, axis=1).astype(jnp.bfloat16)
             c = at[axis_c]
             for by in (1, -1, 2, 0):
                 c_to = step_on(c, by)
@@ -228,20 +286,21 @@
                         remote(box, slot, row_send.at[g, kind], row_recv.at[g, order],
                                moved(at, axis_c, by, core_to, axis_b, by_b))
 
+    def bring(g, order):
+        await_bytes(inbox[g].at[order], row_recv.at[g, order])
+        local_copy(inbox[g].at[order], stage.at[g % 2, :, :, :, :, pl.ds(0, HALF[g])], stage_sem.at[g % 2])
+
     def multiply(g, order):
         axis_a, axis_b, axis_c = ROLES[g]
         b_from = step_on(at[axis_b], STEPS[order])
-        await_bytes(inbox[g].at[order], row_recv.at[g, order])
-        copy = pltpu.make_async_copy(inbox[g].at[order], stage.at[:, :, :, :, pl.ds(0, HALF[g])], stage_sem.at[0])
-        copy.start()
-        copy.wait()
+        await_bytes(stage.at[g % 2, :, :, :, :, pl.ds(0, HALF[g])], stage_sem.at[g % 2])
 
         @pl.loop(0, 2 * HID // 256)
         def _(tile):
             columns = pl.ds(pl.multiple_of(tile * 256, 256), 256)
             total = None
             for h in range(2):
-                rows = stage[h, :, :, :, 0 : HALF[g]].reshape(384, HALF[g])
+                rows = stage[g % 2, h, :, :, :, 0 : HALF[g]].reshape(384, HALF[g])
                 part = jnp.dot(rows, weights[START[g] + h * HALF[g] : START[g] + (h + 1) * HALF[g], columns],
                                preferred_element_type=jnp.float32)
                 total = part if total is None else total + part
@@ -269,7 +328,10 @@
         local_copy(down_w.at[0, :, pl.ds(START[g], WIDTH[g])], down_of(g), w_sem.at[2 + g])
 
     for order in (0, 3, 1, 2):
-        for g in groups:
+        bring(0, order)
+        for g in groups:
+            if g < 2:
+                bring(g + 1, order)
             multiply(g, order)
             if order == 2 and g == 0:
                 fetch_down(0)
@@ -302,22 +364,19 @@
             ]
             rows_bf[c * 96 : (c + 1) * 96, :] = jnp.concatenate(units, axis=0).astype(jnp.bfloat16)
 
-        @pl.loop(0, 2)
-        def _(h):
+        c = at[axis_c]
+        for k in range(2):
+            core_to = (core + k) % 2
             for low_at, size in tiles(HALF[g]):
-                columns = pl.ds(pl.multiple_of(h * HALF[g] + low_at, 128), size)
+                columns = pl.ds(pl.multiple_of(core_to * HALF[g] + low_at, 128), size)
                 made = jnp.dot(rows_bf[...], weights[g * HID : (g + 1) * HID, columns], preferred_element_type=jnp.float32)
                 made = made.astype(jnp.bfloat16).reshape(SIDE, 2, 48, size)
                 for pair in range(2):
-                    outbox[g][order * 2 + pair, pl.ds(h * SIDE, SIDE), :, low_at : low_at + size] = made[:, pair]
-
-        c = at[axis_c]
-        for pair in range(2):
-            kind, by_b = RETURNS[order, pair]
-            for by in (1, -1, 2, 0):
-                c_to = step_on(c, by)
-                for k in range(2):
-                    core_to = (core + k) % 2
+                    outbox[g][order * 2 + pair, pl.ds(core_to * SIDE, SIDE), :, low_at : low_at + size] = made[:, pair]
+            for pair in range(2):
+                kind, by_b = RETURNS[order, pair]
+                for by in (1, -1, 2, 0):
+                    c_to = step_on(c, by)
                     box = outbox[g].at[order * 2 + pair, core_to * SIDE + c_to]
                     slot = backbox[g].at[kind // 2, pair, kind % 2, c * 2 + core]
                     sem = back_recv.at[g, kind // 2, pair]
@@ -326,34 +385,32 @@
                     else:
                         remote(box, slot, back_send.at[g, order, pair], sem, moved(at, axis_c, by, core_to, axis_b, by_b))
 
-    def load(source, target, sem):
-        copy = pltpu.make_async_copy(source, target, sem)
-        copy.start()
-        copy.wait()
-
     def combine(g, is_near, place):
-        view = stage.reshape(2, 8, 48, WIDE).at[:, :, :, pl.ds(0, HALF[g])]
+        wide = pl.ds(0, HALF[g])
+        views = stage.reshape(2, 2, 8, 48, WIDE).at[:, :, :, :, wide]
+        for pair in range(2):
+            await_bytes(backbox[g].at[int(is_near), pair], back_recv.at[g, int(is_near), pair])
+            local_copy(backbox[g].at[int(is_near), pair], views.at[pair], stage_sem.at[pair])
+            if not is_near:
+                await_bytes(landed[g].at[pair], sum_recv.at[g, pair])
+                local_copy(landed[g].at[pair], low.at[pair, :, :, :, wide], stage_sem.at[2 + pair])
 
         @pl.loop(0, 2)
         def _(pair):
             ahead = 1 - 2 * pair
-            codes = column_codes(g, is_near, pair)
-            scale = jnp.concatenate(
-                [meta_of(g, is_near, pair, i, k)[TOPK:] for i in range(2) for k in range(2)], axis=1
-            )
+            number = lax.broadcasted_iota(jnp.int32, (48, 2 * TOK), 0).astype(jnp.float32)
             for side, by in enumerate((0, ahead if is_near else -ahead)):
-                rows = pattern[g] + line_base(g, by)
-                total = jnp.where(rows == codes[0:1], scale[0:1], 0.0)
-                for k in range(1, TOPK):
-                    total = jnp.where(rows == codes[k : k + 1], scale[k : k + 1], total)
-                share[:, side * 384 : (side + 1) * 384] = total.T.astype(jnp.bfloat16)
-            await_bytes(backbox[g].at[int(is_near), pair], back_recv.at[g, int(is_near), pair])
-            load(backbox[g].at[int(is_near), pair], view, stage_sem.at[0])
+                for i in range(2):
+                    slot, weight = slot_rows(g, is_near, pair, i, by)
+                    slot = slot + float(i * UNIT)
+                    found = [jnp.where(number == slot[d : d + 1], weight[d : d + 1], 0.0) for d in range(8)]
+                    total = jnp.concatenate(found, axis=0).T.astype(jnp.bfloat16)
+                    share[i * 256 : (i + 1) * 256, side * 384 : (side + 1) * 384] = total
+            await_bytes(views.at[pair], stage_sem.at[pair])
             if not is_near:
-                await_bytes(landed[g].at[pair], sum_recv.at[g, pair])
-                load(landed[g].at[pair], low.at[:, :, :, pl.ds(0, HALF[g])], stage_sem.at[1])
+                await_bytes(low.at[pair, :, :, :, wide], stage_sem.at[2 + pair])
             for low_at, size in tiles(HALF[g]):
-                block = stage[:, :, :, :, low_at : low_at + size].reshape(768, size)
+                block = stage[pair, :, :, :, :, low_at : low_at + size].reshape(768, size)
                 mixed = jnp.dot(share[...], block, preferred_element_type=jnp.float32)
                 place(pair, low_at, size, mixed.reshape(2, 2, TOK, size))
 
@@ -383,7 +440,7 @@
             for i in range(2):
                 for half in range(2):
                     ref, rows, column = own_at(g, pair * 2 + i, half)
-                    value = block[i, half] + low[i, half, :, low_at : low_at + size].astype(jnp.float32)
+                    value = block[i, half] + low[pair, i, half, :, low_at : low_at + size].astype(jnp.float32)
                     ref[rows, column + low_at : column + low_at + size] = value
 
         combine(g, False, place)
@@ -423,10 +480,11 @@
         pass_on(g)
     for g in groups:
         for way in range(2):
-            await_bytes(gathered[g].at[0], a_send.at[g, way])
+            for half in range(2):
+                await_bytes(gathered[g].at[0, 0], a_send.at[g, way, half])
             await_bytes(gathered[g].at[0, 0], ah_send.at[g, way])
-        for order in range(4):
-            await_bytes(gathered[g].at[0], b_send.at[g, order])
+        for order in range(5):
+            await_bytes(gathered[g].at[0] if order in (1, 2, 3) else gathered[g].at[0, 0], b_send.at[g, order])
     home(0)
     home(1)
     relay(0)
@@ -457,33 +515,20 @@
         await_bytes(ends[g], end_send.at[g])
 
 
-def row_pattern():
-    row = np.arange(384)
-    line, core, inner = row // 96, row // 48 % 2, row % 48
+def line_table():
+    expert = np.arange(8)
     tables = []
     for roles in ROLES:
-        spot = {"x": 0 * line, "y": 0 * line, "z": 0 * line, "core": core}
-        spot[roles[2]] = line
+        spot = {"x": 0 * expert, "y": 0 * expert, "z": 0 * expert, "core": expert % 2}
+        spot[roles[2]] = expert // 2
         node, local = device(spot)
-        tables.append(((node * 8 + local) * SLOTS + inner % SLOTS) * 4 + inner // SLOTS)
+        tables.append((node * 8 + local) * SLOTS)
     return jnp.asarray(np.stack(tables)[:, :, None].astype(np.float32))
 
 
 def body(tokens, norm_gain, routes, route_gates, placement, gate_weight, up_weight, down_weight):
-    experts = placement.shape[0]
-    blocks = TOK // BLOCK_TOK
     bf16, f32 = jnp.bfloat16, jnp.float32
-    combine_weight = (route_gates / jnp.sum(route_gates, axis=-1, keepdims=True)).astype(bf16)
-    expert_ids = jnp.arange(experts, dtype=jnp.int32)
-    holder = jnp.sum(jnp.where(placement[None, :] == expert_ids[:, None], expert_ids[None, :], 0), axis=1)
-    one_hot = routes[:, :, None] == expert_ids
-    target = jnp.sum(jnp.where(one_hot, holder, 0), axis=-1)
-    named = jnp.any(one_hot, axis=1).astype(f32).reshape(blocks, BLOCK_TOK, experts)
-    before = jnp.einsum("ts,bse->bte", jnp.tril(jnp.ones((BLOCK_TOK, BLOCK_TOK), f32), -1), named)
-    position_in = jnp.sum(jnp.where(one_hot, before.reshape(TOK, 1, experts), 0.0), axis=-1)
-    block = (jnp.arange(TOK) // BLOCK_TOK).astype(f32)[:, None]
-    code = target.astype(f32) * SLOTS + block * CAP + position_in
-    own_meta = jnp.concatenate([code.T, combine_weight.astype(f32).T], axis=0)
+    packed = jnp.concatenate([routes.astype(f32), route_gates], axis=1).T
 
     vmem, hbm = pl.BlockSpec(memory_space=pltpu.VMEM), pl.BlockSpec(memory_space=pltpu.HBM)
     dma = pltpu.SemaphoreType.DMA
@@ -499,7 +544,7 @@
         + [shape((4, 2, SIDE, 2, 48, h), bf16) for h in HALF]
         + [shape((2, 2, 2, 8, 48, h), bf16) for h in HALF]
         + [shape((2, 2, 2, TOK, h), bf16) for h in HALF],
-        in_specs=[vmem] * 4 + [hbm] * 3,
+        in_specs=[vmem] * 6 + [hbm] * 3,
         out_specs=[vmem] + [hbm] * 9,
         scratch_shapes=each(SIDE, 2, TOK)
         + each(2, 2, 2, TOK)
@@ -508,26 +553,27 @@
         + [pltpu.VMEM((SIDE, *meta), f32)] * 3
         + [pltpu.VMEM((2, 2, *meta), f32)] * 3
         + [
-            pltpu.VMEM((2, SIDE, 2, 48, WIDE), bf16),
+            pltpu.VMEM((2 * TOPK, TOK), f32),
+            pltpu.VMEM((2, 2, SIDE, 2, 48, WIDE), bf16),
             pltpu.VMEM((512, 768), bf16),
             pltpu.VMEM((384, HID), bf16),
             pltpu.VMEM((D, 2 * HID), bf16),
             pltpu.VMEM((64 * UNIT, 2 * HID), f32),
             pltpu.VMEM((SIDE * 2 * TOK, HALF[2]), f32),
-            pltpu.VMEM((2, 2, TOK, WIDE), bf16),
+            pltpu.VMEM((2, 2, 2, TOK, WIDE), bf16),
         ]
         + each(6, TOK)
         + [pltpu.VMEM((2, TOK, D // 2), bf16)]
         + each(TOK)
         + [
             dma((5,)), dma((3,)), dma((3,)), dma((3,)), dma((3, 3)), dma((3, 3)),
-            dma((3, 2)), dma((3, 2)), dma((3, 2)), dma((3, 2)), dma((3, 4)), dma((3, 2)),
-            dma((3, 4)), dma((3, 4)), dma((2,)), dma((3, 4, 2)), dma((3, 2, 2)), dma((3, 2)), dma((3, 2)),
+            dma((3, 2, 2)), dma((3, 2, 2)), dma((3, 2)), dma((3, 2)), dma((3, 5)), dma((3, 2)),
+            dma((3, 4)), dma((3, 4)), dma((4,)), dma((3, 4, 2)), dma((3, 2, 2)), dma((3, 2)), dma((3, 2)),
             dma((3, 4)), dma((3, 4)), dma((3,)), dma((3,)),
         ],
         compiler_params=pltpu.CompilerParams(collective_id=0, has_side_effects=True, vmem_limit_bytes=VMEM_LIMIT),
         name="experts",
-    )(tokens, norm_gain[None, :], own_meta, row_pattern(), gate_weight, up_weight, down_weight)
+    )(tokens, norm_gain[None, :], routes, packed, placement[None, :], line_table(), gate_weight, up_weight, down_weight)
     return result
 
 

time: 322 us -> 279 us (0.87); the launches traced: 318 us -> 279 us
  Pallas kernels: 307 us -> 272 us
  other arithmetic: 5.82 us -> 1.97 us
    pallas_call x1, Pallas kernels: 307 us -> 272 us  [body(): pl.pallas_call(kernel, out_shape=[shape((TOK, D), bf16)] + [shape((4, 2,...]
    reduce_sum x4 -> x0, other arithmetic: 4.24 us -> none  [the longest x1 2.41 us: body(): target = jnp.sum(jnp.where(one_hot, holder, 0), axis=-1)]
where the time goes in v1:
time: 279 us
  Pallas kernels  272 us (97%)
  local copies, waits for them, and re-layouts  5 us (2%)
    pallas_call x1, Pallas kernels, body(): pl.pallas_call(kernel, out_shape=[shape((TOK, D), bf16)] + [shape((4, 2,...  272 us

profile of v1, /device:TPU:35, one launch (start us, length us, event | category | flops | bytes accessed | tf_op | source)
XLA Modules:
  0.0 279.0 jit_solution(6292389515884511348)
XLA Ops:
  0.0 0.7 convert_element_type.3
  0.7 1.3 maximum_bitcast_fusion.packed
  2.0 1.3 broadcast_in_dim.6.gain
  3.3 1.4 copy.10.routes
  4.7 272.0 %experts.1 = (bf16[128,4096]{1,0:T(8,128)(2,1)}, bf16[4,2,4,2,48,768]{5,4,3,2,1,0:T(8,128)(2,1)}, bf16[4,2,4,2,48,640]{5,4,3,2,1,0:T(8,128)(2,1)}, bf16[4,2,4,2,...) custom-call(bf16[128,4096]{1,0:T(8,128)(2,1)} %tokens.1, ...), custom_call_target="tpu_custom_call" | custom-call | tf_op jit(solution)/shard_map/experts/pallas_call | solution.py:541
  276.7 2.3 copy.12

commit v2 on v1

--- a/solution.py
+++ b/solution.py
@@ -31,6 +31,8 @@
     (3, 0): (3, -1), (3, 1): (3, 1),
 }
 VMEM_LIMIT = 62 << 20
+MIX = 768
+EXP = 768
 
 
 def position():
@@ -90,38 +92,43 @@
     pltpu.make_async_copy(ref, ref, sem).wait()
 
 
+def mix_tiles(width):
+    return [(at, min(MIX, width - at)) for at in range(0, width, MIX)]
+
+
 def tiles(width):
-    return [(at, min(256, width - at)) for at in range(0, width, 256)]
-
-
-def slot_codes(routes, packed, placement):
+    return [(at, min(EXP, width - at)) for at in range(0, width, EXP)]
+
+
+def slot_codes(packed, placement):
     side = (TOK, TOK)
     down = lax.broadcasted_iota(jnp.int32, side, 0)
     across = lax.broadcasted_iota(jnp.int32, side, 1)
     earlier = jnp.logical_and(down < across, down // BLOCK_TOK == across // BLOCK_TOK)
     place = jnp.broadcast_to(placement[...].astype(jnp.float32), side).T
     index = down.astype(jnp.float32)
-    columns = [jnp.broadcast_to(routes[:, k : k + 1].astype(jnp.float32), side) for k in range(TOPK)]
+    columns = [jnp.broadcast_to(packed[:, k : k + 1], side) for k in range(TOPK)]
+    table = packed[...].T
     block = (across[0:1] // BLOCK_TOK * CAP).astype(jnp.float32)
     codes = []
     for k in range(TOPK):
-        wanted = packed[k : k + 1]
+        wanted = table[k : k + 1]
         holder = jnp.sum(jnp.where(place == wanted, index, 0.0), axis=0, keepdims=True)
         same = columns[0] == wanted
         for column in columns[1:]:
             same = jnp.logical_or(same, column == wanted)
         count = jnp.sum(jnp.where(jnp.logical_and(same, earlier), 1.0, 0.0), axis=0, keepdims=True)
         codes.append(holder * float(SLOTS) + block + count)
-    gates = packed[TOPK:]
+    gates = table[TOPK : 2 * TOPK]
     weight = gates / jnp.sum(gates, axis=0, keepdims=True)
     return jnp.concatenate(codes + [weight.astype(jnp.bfloat16).astype(jnp.float32)], axis=0)
 
 
 def kernel(
-    tokens, gain, routes, packed, placement, lines, gate_w, up_w, down_w,
+    tokens, gain, packed, placement, lines, gate_w, up_w, down_w,
     result, in0, in1, in2, back0, back1, back2, land0, land1, land2,
     g0, g1, g2, n0, n1, n2, out0, out1, out2, st0, st1, st2, m0, m1, m2, k0, k1, k2,
-    code_box, stage, share, rows_bf, weights, acc, own2, low, r0, r1, r2, last, end0, end1, end2,
+    code_box, stage, lot, share, rows_bf, weights, acc, own2, low, r0, r1, r2, last, end0, end1, end2,
     w_sem, own_sem, core_send, core_recv, meta_send, meta_recv, a_send, a_recv, ah_send, ah_recv, b_send, b_recv,
     row_send, row_recv, stage_sem, back_send, back_recv, sum_send, sum_recv, c_send, c_recv, end_send, end_recv,
 ):
@@ -177,7 +184,7 @@
         ring(g, core, True)
     for g in groups:
         spread_own(g, core, True)
-    code_box[...] = slot_codes(routes, packed, placement)
+    code_box[...] = slot_codes(packed, placement)
     for g in groups:
         a = at[ROLES[g][0]]
         metas[g][a, core] = code_box[...]
@@ -254,7 +261,7 @@
 
         @pl.loop(0, 2)
         def _(pair):
-            if kind == 3:
+            if kind == 2:
                 await_bytes(near[g].at[pair], b_recv.at[g, pair])
             ahead = 1 - 2 * pair
             by_b = (0, -ahead, 0, ahead)[kind]
@@ -288,22 +295,19 @@
 
     def bring(g, order):
         await_bytes(inbox[g].at[order], row_recv.at[g, order])
-        local_copy(inbox[g].at[order], stage.at[g % 2, :, :, :, :, pl.ds(0, HALF[g])], stage_sem.at[g % 2])
+        for h in range(2):
+            local_copy(inbox[g].at[order, h], stage.at[g % 2, :, :, :, pl.ds(h * HALF[g], HALF[g])], stage_sem.at[g % 2])
 
     def multiply(g, order):
         axis_a, axis_b, axis_c = ROLES[g]
         b_from = step_on(at[axis_b], STEPS[order])
-        await_bytes(stage.at[g % 2, :, :, :, :, pl.ds(0, HALF[g])], stage_sem.at[g % 2])
-
-        @pl.loop(0, 2 * HID // 256)
+        await_bytes(stage.at[g % 2, :, :, :, pl.ds(0, WIDTH[g])], stage_sem.at[g % 2])
+
+        @pl.loop(0, 2)
         def _(tile):
-            columns = pl.ds(pl.multiple_of(tile * 256, 256), 256)
-            total = None
-            for h in range(2):
-                rows = stage[g % 2, h, :, :, :, 0 : HALF[g]].reshape(384, HALF[g])
-                part = jnp.dot(rows, weights[START[g] + h * HALF[g] : START[g] + (h + 1) * HALF[g], columns],
-                               preferred_element_type=jnp.float32)
-                total = part if total is None else total + part
+            columns = pl.ds(pl.multiple_of(tile * HID, 256), HID)
+            rows = stage[g % 2, :, :, :, 0 : WIDTH[g]].reshape(384, WIDTH[g])
+            total = jnp.dot(rows, weights[START[g] : START[g] + WIDTH[g], columns], preferred_element_type=jnp.float32)
             for c in range(SIDE):
                 for a in range(SIDE):
                     unit = a * STRIDE[axis_a] + b_from * STRIDE[axis_b] + c * STRIDE[axis_c]
@@ -315,7 +319,7 @@
             pick_and_send(g, kind)
     for g in groups:
         await_bytes(near_metas[g], meta_recv.at[g, 2])
-    for kind in (3, 2):
+    for kind in (2, 3):
         for g in groups:
             pick_and_send(g, kind)
     await_bytes(weights.at[:, pl.ds(0, HID)], w_sem.at[0])
@@ -327,16 +331,16 @@
     def fetch_down(g):
         local_copy(down_w.at[0, :, pl.ds(START[g], WIDTH[g])], down_of(g), w_sem.at[2 + g])
 
-    for order in (0, 3, 1, 2):
+    for order in (0, 1, 2, 3):
         bring(0, order)
         for g in groups:
             if g < 2:
                 bring(g + 1, order)
             multiply(g, order)
-            if order == 2 and g == 0:
+            if order == 3 and g == 0:
                 fetch_down(0)
                 fetch_down(1)
-            if order == 2 and g == 1:
+            if order == 3 and g == 1:
                 fetch_down(2)
 
     @pl.loop(0, 64)
@@ -385,9 +389,24 @@
                     else:
                         remote(box, slot, back_send.at[g, order, pair], sem, moved(at, axis_c, by, core_to, axis_b, by_b))
 
+    def build_share(g, is_near, pair, target):
+        ahead = 1 - 2 * pair
+        number = lax.broadcasted_iota(jnp.int32, (48, 2 * TOK), 0).astype(jnp.float32)
+        for side, by in enumerate((0, ahead if is_near else -ahead)):
+            for i in range(2):
+                slot, weight = slot_rows(g, is_near, pair, i, by)
+                slot = slot + float(i * UNIT)
+                found = [jnp.where(number == slot[d : d + 1], weight[d : d + 1], 0.0) for d in range(8)]
+                ref, at_row, at_column = target
+                total = jnp.concatenate(found, axis=0).T.astype(jnp.bfloat16)
+                ref[at_row + i * 256 : at_row + (i + 1) * 256, pl.ds(at_column + side * 384, 384)] = total
+
+    def home_share(g, pair):
+        return weights, 3 * HID + g * 512, pl.multiple_of(pair * 768, 128)
+
     def combine(g, is_near, place):
         wide = pl.ds(0, HALF[g])
-        views = stage.reshape(2, 2, 8, 48, WIDE).at[:, :, :, :, wide]
+        views = lot.at[:, :, :, :, wide]
         for pair in range(2):
             await_bytes(backbox[g].at[int(is_near), pair], back_recv.at[g, int(is_near), pair])
             local_copy(backbox[g].at[int(is_near), pair], views.at[pair], stage_sem.at[pair])
@@ -397,21 +416,19 @@
 
         @pl.loop(0, 2)
         def _(pair):
-            ahead = 1 - 2 * pair
-            number = lax.broadcasted_iota(jnp.int32, (48, 2 * TOK), 0).astype(jnp.float32)
-            for side, by in enumerate((0, ahead if is_near else -ahead)):
-                for i in range(2):
-                    slot, weight = slot_rows(g, is_near, pair, i, by)
-                    slot = slot + float(i * UNIT)
-                    found = [jnp.where(number == slot[d : d + 1], weight[d : d + 1], 0.0) for d in range(8)]
-                    total = jnp.concatenate(found, axis=0).T.astype(jnp.bfloat16)
-                    share[i * 256 : (i + 1) * 256, side * 384 : (side + 1) * 384] = total
+            if is_near:
+                build_share(g, True, pair, (share, 0, 0))
             await_bytes(views.at[pair], stage_sem.at[pair])
             if not is_near:
                 await_bytes(low.at[pair, :, :, :, wide], stage_sem.at[2 + pair])
-            for low_at, size in tiles(HALF[g]):
-                block = stage[pair, :, :, :, :, low_at : low_at + size].reshape(768, size)
-                mixed = jnp.dot(share[...], block, preferred_element_type=jnp.float32)
+            for low_at, size in mix_tiles(HALF[g]):
+                block = lot[pair, :, :, :, low_at : low_at + size].reshape(768, size)
+                if is_near:
+                    shares = share[...]
+                else:
+                    ref, at_row, at_column = home_share(g, pair)
+                    shares = ref[at_row : at_row + 512, pl.ds(at_column, 768)]
+                mixed = jnp.dot(shares, block, preferred_element_type=jnp.float32)
                 place(pair, low_at, size, mixed.reshape(2, 2, TOK, size))
 
     def pass_on(g):
@@ -449,19 +466,21 @@
             gathered[g][0, half] = settled(g, opposite, half).astype(jnp.bfloat16)
             remote(gathered[g].at[0, half], arrived[g].at[half], c_send.at[g, half], c_recv.at[g, half],
                    moved(at, axis_a, by))
+        for half_in, by in enumerate((1, -1)):
+            half = 1 - half_in
+            gathered[g][1 + half_in, half] = settled(g, step_on(at[axis_a], by), half).astype(jnp.bfloat16)
+            pass_half(g, half_in, half, by)
+
+    def pass_half(g, half_in, half, by):
+        remote(gathered[g].at[1 + half_in, half], arrived[g].at[2 + 2 * half_in + half], c_send.at[g, 2 + half_in],
+               c_recv.at[g, 2 + half_in], moved(at, ROLES[g][0], by))
 
     def relay(g):
-        axis_a = ROLES[g][0]
         for half_in, by in enumerate((1, -1)):
-            a_to = step_on(at[axis_a], by)
             await_bytes(arrived[g].at[half_in], c_recv.at[g, half_in])
-            for half in range(2):
-                value = settled(g, a_to, half)
-                if half == half_in:
-                    value = value + arrived[g][half_in].astype(jnp.float32)
-                gathered[g][1 + half_in, half] = value.astype(jnp.bfloat16)
-            remote(gathered[g].at[1 + half_in], arrived[g].at[pl.ds(2 + 2 * half_in, 2)], c_send.at[g, 2 + half_in],
-                   c_recv.at[g, 2 + half_in], moved(at, axis_a, by))
+            value = settled(g, step_on(at[ROLES[g][0]], by), half_in) + arrived[g][half_in].astype(jnp.float32)
+            gathered[g][1 + half_in, half_in] = value.astype(jnp.bfloat16)
+            pass_half(g, half_in, half_in, by)
 
     def finish(g):
         for index in range(2):
@@ -476,6 +495,12 @@
     for order in (3, 1, 2, 0):
         for g in groups:
             expand_and_send(g, order)
+    for g in groups:
+
+        @pl.loop(0, 2)
+        def _(pair):
+            build_share(g, False, pair, home_share(g, pair))
+
     for g in groups:
         pass_on(g)
     for g in groups:
@@ -528,7 +553,7 @@
 
 def body(tokens, norm_gain, routes, route_gates, placement, gate_weight, up_weight, down_weight):
     bf16, f32 = jnp.bfloat16, jnp.float32
-    packed = jnp.concatenate([routes.astype(f32), route_gates], axis=1).T
+    packed = jnp.concatenate([routes.astype(f32), route_gates, jnp.zeros((TOK, TOK - 2 * TOPK), f32)], axis=1)
 
     vmem, hbm = pl.BlockSpec(memory_space=pltpu.VMEM), pl.BlockSpec(memory_space=pltpu.HBM)
     dma = pltpu.SemaphoreType.DMA
@@ -544,7 +569,7 @@
         + [shape((4, 2, SIDE, 2, 48, h), bf16) for h in HALF]
         + [shape((2, 2, 2, 8, 48, h), bf16) for h in HALF]
         + [shape((2, 2, 2, TOK, h), bf16) for h in HALF],
-        in_specs=[vmem] * 6 + [hbm] * 3,
+        in_specs=[vmem] * 5 + [hbm] * 3,
         out_specs=[vmem] + [hbm] * 9,
         scratch_shapes=each(SIDE, 2, TOK)
         + each(2, 2, 2, TOK)
@@ -554,7 +579,8 @@
         + [pltpu.VMEM((2, 2, *meta), f32)] * 3
         + [
             pltpu.VMEM((2 * TOPK, TOK), f32),
-            pltpu.VMEM((2, 2, SIDE, 2, 48, WIDE), bf16),
+            pltpu.VMEM((2, SIDE, 2, 48, 2 * WIDE), bf16),
+            pltpu.VMEM((2, 2, 8, 48, WIDE), bf16),
             pltpu.VMEM((512, 768), bf16),
             pltpu.VMEM((384, HID), bf16),
             pltpu.VMEM((D, 2 * HID), bf16),
@@ -573,7 +599,7 @@
         ],
         compiler_params=pltpu.CompilerParams(collective_id=0, has_side_effects=True, vmem_limit_bytes=VMEM_LIMIT),
         name="experts",
-    )(tokens, norm_gain[None, :], routes, packed, placement[None, :], line_table(), gate_weight, up_weight, down_weight)
+    )(tokens, norm_gain[None, :], packed, placement[None, :], line_table(), gate_weight, up_weight, down_weight)
     return result
 
 

time: 279 us -> 265 us (0.950)
  Pallas kernels: 272 us -> 256 us
    pallas_call x1, Pallas kernels: 272 us -> 256 us  [body(): pl.pallas_call(kernel, out_shape=[shape((TOK, D), bf16)] + [shape((4, 2,...]
where the time goes in v2:
time: 265 us; the launch traced here: 262 us
  Pallas kernels  256 us (97%)
  local copies, waits for them, and re-layouts  4.55 us (2%)
    pallas_call x1, Pallas kernels, body(): pl.pallas_call(kernel, out_shape=[shape((TOK, D), bf16)] + [shape((4, 2,...  256 us

profile of v2, /device:TPU:35, one launch (start us, length us, event | category | flops | bytes accessed | tf_op | source)
XLA Modules:
  0.0 262.4 jit_solution(10628713009220406389)
XLA Ops:
  0.0 0.1 pad.2.clone
  0.1 0.7 convert_element_type.3
  0.8 1.3 broadcast_in_dim.9.gain
  2.1 0.1 copy.10
  2.2 0.8 copy.11
  3.0 0.7 maximum_maximum_fusion.packed
  3.7 256.4 %experts.1 = (bf16[128,4096]{1,0:T(8,128)(2,1)}, bf16[4,2,4,2,48,768]{5,4,3,2,1,0:T(8,128)(2,1)}, bf16[4,2,4,2,48,640]{5,4,3,2,1,0:T(8,128)(2,1)}, bf16[4,2,4,2,...) custom-call(bf16[128,4096]{1,0:T(8,128)(2,1)} %tokens.1, ...), custom_call_target="tpu_custom_call" | custom-call | tf_op jit(solution)/shard_map/experts/pallas_call | solution.py:566
  260.1 2.3 copy.13
  (1 shorter events, 0.0 us)

commit v3 on v2

--- a/solution.py
+++ b/solution.py
@@ -368,7 +368,6 @@
             ]
             rows_bf[c * 96 : (c + 1) * 96, :] = jnp.concatenate(units, axis=0).astype(jnp.bfloat16)
 
-        c = at[axis_c]
         for k in range(2):
             core_to = (core + k) % 2
             for low_at, size in tiles(HALF[g]):
@@ -378,16 +377,23 @@
                 for pair in range(2):
                     outbox[g][order * 2 + pair, pl.ds(core_to * SIDE, SIDE), :, low_at : low_at + size] = made[:, pair]
             for pair in range(2):
-                kind, by_b = RETURNS[order, pair]
-                for by in (1, -1, 2, 0):
-                    c_to = step_on(c, by)
-                    box = outbox[g].at[order * 2 + pair, core_to * SIDE + c_to]
-                    slot = backbox[g].at[kind // 2, pair, kind % 2, c * 2 + core]
-                    sem = back_recv.at[g, kind // 2, pair]
-                    if by == 0 and k == 0 and by_b == 0:
-                        local_copy(box, slot, sem)
-                    else:
-                        remote(box, slot, back_send.at[g, order, pair], sem, moved(at, axis_c, by, core_to, axis_b, by_b))
+                if RETURNS[order, pair][0] != 1:
+                    send_back(g, order, pair, k)
+
+    def send_back(g, order, pair, k):
+        _, axis_b, axis_c = ROLES[g]
+        c = at[axis_c]
+        core_to = (core + k) % 2
+        kind, by_b = RETURNS[order, pair]
+        for by in (1, -1, 2, 0):
+            c_to = step_on(c, by)
+            box = outbox[g].at[order * 2 + pair, core_to * SIDE + c_to]
+            slot = backbox[g].at[kind // 2, pair, kind % 2, c * 2 + core]
+            sem = back_recv.at[g, kind // 2, pair]
+            if by == 0 and k == 0 and by_b == 0:
+                local_copy(box, slot, sem)
+            else:
+                remote(box, slot, back_send.at[g, order, pair], sem, moved(at, axis_c, by, core_to, axis_b, by_b))
 
     def build_share(g, is_near, pair, target):
         ahead = 1 - 2 * pair
@@ -492,7 +498,7 @@
         span = pl.ds(START[g] // 2, HALF[g])
         remote(last.at[other, :, span], ends[g], end_send.at[g], end_recv.at[g], moved(at, "x", 0, other))
 
-    for order in (3, 1, 2, 0):
+    for order in (3, 1, 2):
         for g in groups:
             expand_and_send(g, order)
     for g in groups:
@@ -502,7 +508,12 @@
             build_share(g, False, pair, home_share(g, pair))
 
     for g in groups:
+        for k in range(2):
+            send_back(g, 1, 1, k)
+            send_back(g, 2, 0, k)
+    for g in groups:
         pass_on(g)
+        expand_and_send(g, 0)
     for g in groups:
         for way in range(2):
             for half in range(2):

time: 265 us -> 254 us (0.958)
  Pallas kernels: 256 us -> 245 us
    pallas_call x1, Pallas kernels: 256 us -> 245 us  [body(): pl.pallas_call(kernel, out_shape=[shape((TOK, D), bf16)] + [shape((4, 2,...]
where the time goes in v3:
time: 254 us; the launch traced here: 251 us
  Pallas kernels  245 us (96%)
  local copies, waits for them, and re-layouts  4.55 us (2%)
    pallas_call x1, Pallas kernels, body(): pl.pallas_call(kernel, out_shape=[shape((TOK, D), bf16)] + [shape((4, 2,...  245 us

profile of v3, /device:TPU:35, one launch (start us, length us, event | category | flops | bytes accessed | tf_op | source)
XLA Modules:
  0.0 251.2 jit_solution(2532154050354846703)
XLA Ops:
  0.0 0.1 pad.2.clone
  0.1 0.7 convert_element_type.3
  0.8 1.3 broadcast_in_dim.9.gain
  2.1 0.1 copy.10
  2.2 0.8 copy.11
  3.0 0.7 maximum_maximum_fusion.packed
  3.7 245.2 %experts.1 = (bf16[128,4096]{1,0:T(8,128)(2,1)}, bf16[4,2,4,2,48,768]{5,4,3,2,1,0:T(8,128)(2,1)}, bf16[4,2,4,2,48,640]{5,4,3,2,1,0:T(8,128)(2,1)}, bf16[4,2,4,2,...) custom-call(bf16[128,4096]{1,0:T(8,128)(2,1)} %tokens.1, ...), custom_call_target="tpu_custom_call" | custom-call | tf_op jit(solution)/shard_map/experts/pallas_call | solution.py:577
  248.9 2.3 copy.13
  (1 shorter events, 0.0 us)
